TPU v7x, 128 devices: a whole 4x4x4 slice. The times are simulated.
128 devices in a mesh: engine: 16 (over x, z), tp: 8 (over y, core).
Axes of the slice: x: 4, y: 4, z: 4, core: 2. Of those that a mesh axis runs over, the one named last changes fastest.
Arguments:
- kv_pool: bfloat16 [1792, 8, 128, 256], P('engine', 'tp'), may hold values from -6 to 6
- page_table: int32 [256, 7], P('engine'), may hold values from 0 to 111, as said below
- hist_len: int32 [256], replicated, may hold values from 1 to 895, as said below
- new_slot: int32 [256], replicated, may hold values from 0 to 255, as said below
- dec_q: bfloat16 [256, 8192], P('engine', 'tp'), may hold values from -6 to 6
- dec_kv: bfloat16 [256, 8, 256], P('engine', 'tp'), may hold values from -6 to 6
- tool_q: bfloat16 [8192, 8192], P('engine', 'tp'), may hold values from -6 to 6
- tool_kv: bfloat16 [8192, 8, 256], P('engine', 'tp'), may hold values from -6 to 6
- w_out: bfloat16 [8192, 8192], P('tp'), may hold values from -0.0625 to 0.0625
Outputs:
- dec_out: bfloat16 [256, 8192], P('engine', 'tp')
- tool_out: bfloat16 [8192, 8192], P('engine', 'tp')
Inputs may be any that keep to these rules, and one draw needn't show every extreme that they name: `page_table`: entry [g, p] is a page of the pool of conversation g's engine, rows (g // 16) * 112 onward of kv_pool; the 16 conversations of one engine use each of its 112 pages exactly once. `hist_len`: the largest value is reached in every draw. A permutation; conversation g moves to engine new_slot[g] // 16. Every engine receives exactly 16 conversations; of the conversations of one old engine at most 2 go to the same new engine, and exactly 2 for some pair of engines in every draw.
All inputs are finite; a program needn't handle non-finite values.
Results may differ from a plain program's by a relative error of at most 0.02.
Values may be sent and summed in bfloat16 or wider, within the bound.
A program may use at most 128 MiB of HBM per device.

v0:
```python
import jax
import jax.numpy as jnp
from jax import lax
from jax.sharding import PartitionSpec as P

CAP = 2


def prefix_scores(queries, kv_cache, limit, score_scale):
    head_dim = queries.shape[-1]
    pages_max, page_len = (kv_cache.shape[1], kv_cache.shape[3])
    scores = (
        jnp.einsum(
            "cthgd,cphrd->chgtpr",
            queries,
            kv_cache[..., :head_dim],
            preferred_element_type=jnp.float32,
        )
        * score_scale
    )
    position = jnp.arange(pages_max * page_len, dtype=jnp.int32).reshape(pages_max, page_len)
    live_mask = position[None] <= limit[:, None, None]
    return jnp.where(live_mask[:, None, None, None], scores, -jnp.inf)


def causal_scores(queries, fresh_kv, score_scale):
    head_dim = queries.shape[-1]
    tool_len = queries.shape[1]
    scores = (
        jnp.einsum(
            "cthgd,cuhd->chgtu",
            queries,
            fresh_kv[..., :head_dim],
            preferred_element_type=jnp.float32,
        )
        * score_scale
    )
    tool_order = jnp.arange(tool_len, dtype=jnp.int32)
    causal = tool_order[:, None] >= tool_order[None, :]
    return jnp.where(causal, scores, -jnp.inf)


def local(kv_pool, page_table, hist_len, new_slot, dec_q, dec_kv, tool_q, tool_kv, w_out):
    engines = lax.axis_size("engine")
    engine_id = lax.axis_index("engine")
    conv_dev, pages_max = page_table.shape
    heads_kv, page_len = (kv_pool.shape[1], kv_pool.shape[2])
    head_dim = kv_pool.shape[3] // 2
    group_size = dec_q.shape[1] // (heads_kv * head_dim)
    tool_len = tool_q.shape[0] // conv_dev
    score_scale = head_dim ** (-0.5)
    local_ids = jnp.arange(conv_dev, dtype=jnp.int32)
    all_ids = jnp.arange(engines * conv_dev, dtype=jnp.int32)
    peer_ids = jnp.arange(engines, dtype=jnp.int32)
    slot_ids = jnp.arange(CAP, dtype=jnp.int32)
    position = jnp.arange(pages_max * page_len, dtype=jnp.int32).reshape(pages_max, page_len)
    own_hist = lax.dynamic_slice_in_dim(hist_len, engine_id * conv_dev, conv_dev)
    kv_cache = kv_pool[page_table]
    written = position[None] == own_hist[:, None, None]
    kv_cache = jnp.where(written[:, :, None, :, None], dec_kv[:, None, :, None, :], kv_cache)
    queries = dec_q.reshape(conv_dev, heads_kv, group_size, head_dim)
    scores = (
        jnp.einsum(
            "chgd,cphrd->chgpr",
            queries,
            kv_cache[..., :head_dim],
            preferred_element_type=jnp.float32,
        )
        * score_scale
    )
    live_mask = position[None] <= own_hist[:, None, None]
    scores = jnp.where(live_mask[:, None, None], scores, -jnp.inf)
    row_peak = jnp.max(scores, axis=(3, 4), keepdims=True)
    exponent = jnp.exp(scores - row_peak)
    row_total = jnp.sum(exponent, axis=(3, 4))
    weighted = jnp.einsum(
        "chgpr,cphrd->chgd",
        exponent.astype(jnp.bfloat16),
        kv_cache[..., head_dim:],
        preferred_element_type=jnp.float32,
    )
    dec_attn = (weighted / row_total[..., None]).astype(jnp.bfloat16).reshape(conv_dev, -1)
    target = new_slot // conv_dev
    target_grid = target.reshape(engines, conv_dev)
    before = local_ids[None, :] < local_ids[:, None]
    rank_in = jnp.sum(
        (target_grid[:, :, None] == target_grid[:, None, :]) & before[None], axis=2
    ).reshape(-1)
    my_target = lax.dynamic_slice_in_dim(target, engine_id * conv_dev, conv_dev)
    my_rank = lax.dynamic_slice_in_dim(rank_in, engine_id * conv_dev, conv_dev)
    outgoing = (my_target[None, None, :] == peer_ids[:, None, None]) & (
        my_rank[None, None, :] == slot_ids[None, :, None]
    )
    send_index = jnp.sum(jnp.where(outgoing, local_ids, 0), axis=2)
    holder = new_slot[None, :] == (engine_id * conv_dev + local_ids)[:, None]
    anchor = jnp.sum(jnp.where(holder, all_ids, 0), axis=1)
    anchor_rank = jnp.sum(jnp.where(holder, rank_in, 0), axis=1)
    anchor_hist = jnp.sum(jnp.where(holder, hist_len, 0), axis=1)
    anchor_engine = anchor // conv_dev
    recv_index = anchor_engine * CAP + anchor_rank
    tool_queries = tool_q.reshape(conv_dev, tool_len, heads_kv, group_size, head_dim)
    fresh_kv = tool_kv.reshape(conv_dev, tool_len, heads_kv, 2 * head_dim)
    near_score = causal_scores(tool_queries, fresh_kv, score_scale)
    parcel = kv_cache[send_index]
    arrived = lax.all_to_all(parcel, "engine", split_axis=0, concat_axis=0, tiled=True)
    arrived = arrived.reshape((engines * CAP,) + kv_cache.shape[1:])[recv_index]
    far_score = prefix_scores(tool_queries, arrived, anchor_hist, score_scale)
    row_peak = jnp.maximum(jnp.max(far_score, axis=(4, 5)), jnp.max(near_score, axis=4))
    far_exp = jnp.exp(far_score - row_peak[..., None, None])
    near_exp = jnp.exp(near_score - row_peak[..., None])
    row_total = jnp.sum(far_exp, axis=(4, 5)) + jnp.sum(near_exp, axis=4)
    weighted = jnp.einsum(
        "chgtpr,cphrd->cthgd",
        far_exp.astype(jnp.bfloat16),
        arrived[..., head_dim:],
        preferred_element_type=jnp.float32,
    )
    weighted = weighted + jnp.einsum(
        "chgtu,cuhd->cthgd",
        near_exp.astype(jnp.bfloat16),
        fresh_kv[..., head_dim:],
        preferred_element_type=jnp.float32,
    )
    tool_attn = (
        (weighted / jnp.moveaxis(row_total, 3, 1)[..., None])
        .astype(jnp.bfloat16)
        .reshape(conv_dev * tool_len, -1)
    )
    dec_out = lax.psum_scatter(
        jnp.dot(dec_attn, w_out, preferred_element_type=jnp.float32).astype(jnp.bfloat16),
        "tp",
        scatter_dimension=1,
        tiled=True,
    )
    tool_out = lax.psum_scatter(
        jnp.dot(tool_attn, w_out, preferred_element_type=jnp.float32).astype(jnp.bfloat16),
        "tp",
        scatter_dimension=1,
        tiled=True,
    )
    return (dec_out, tool_out)


def solution(mesh):
    return jax.shard_map(
        local,
        mesh=mesh,
        in_specs=(
            P("engine", "tp", None, None),
            P("engine", None),
            P(),
            P(),
            P("engine", "tp"),
            P("engine", "tp", None),
            P("engine", "tp"),
            P("engine", "tp", None),
            P("tp", None),
        ),
        out_specs=(P("engine", "tp"), P("engine", "tp")),
        check_vma=False,
    )
```

profile of v0, /device:TPU:0, one launch (start us, length us, event | category | flops | bytes accessed | tf_op | source)
XLA Modules:
  0.0 411.6 jit_solution(14334000081226012326)
XLA Ops:
  7.2 0.7 compare_select_fusion.3
  7.9 0.1 copy.32
  8.0 0.1 reshape.326
  8.1 0.7 and_select_fusion.1
  8.8 0.1 eq.81
  8.9 0.1 dynamic_slice.10
  8.9 0.8 dynamic_slice.9
  9.7 0.4 convert_reduce_fusion
  10.1 0.1 reshape.311
  10.2 0.1 dynamic_slice.11
  10.3 0.9 fusion.43
  11.2 0.1 select_reduce_fusion
  11.3 0.1 copy.33
  11.4 0.1 reshape.336
  11.5 0.0 copy-start.3
  11.5 9.4 %gather_fusion = bf16[112,128,256]{2,1,0:T(8,128)(2,1)} fusion(bf16[112,128,256]{2,1,0:T(8,128)(2,1)} %bitcast.194, s32[1024]{0:T(1024)S(1)} %pad_clamp_fusion.2), kind=kCustom, calls=%fused_computation | custom fusion | bytes 14680512 | tf_op jit(solution)/shard_map/gather | solution.py:58
  21.0 0.1 broadcast_compare_fusion.2
  21.1 0.0 copy-done.3
  21.1 7.3 %fusion.51 = bf16[16,7,128,256]{3,2,1,0:T(8,128)(2,1)} fusion(bf16[16,7,1,128,256]{4,3,1,0,2:T(8,128)(2,1)} %bitcast.189, bf16[16,256]{1,0:T(8,128)(2,1)S(1)} %bitcast.202, pred[16,7,128]{2,1,0:T(8,128)(4,1)S(1)} %get-tuple-element.6), kind=kLoop, calls=%fused_computation.95 | loop fusion | flops 3670016 | bytes 14702592 | tf_op jit(solution)/shard_map/jit(_where)/select_n | solution.py:60
  28.4 10.5 %gather_fusion.1 = bf16[32,7,128,256]{3,2,1,0:T(8,128)(2,1)} fusion(bf16[16,7,128,256]{3,2,1,0:T(8,128)(2,1)} %fusion.51, s32[1024]{0:T(1024)S(1)} %pad_clamp_fusion.1), kind=kCustom, calls=%fused_computation.1 | custom fusion | bytes 29360256 | tf_op jit(solution)/shard_map/gather | solution.py:104
  39.0 8.1 %all-to-all-start = ((bf16[16,2,7,1,128,256]{5,4,2,1,3,0:T(8,128)(2,1)}), bf16[16,2,7,1,128,256]{5,4,2,1,3,0:T(8,128)(2,1)}, u32[]{:S(2)}, u32[]{:S(2)}) async-start(bf16[16,2,7,1,128,256]{5,4,2,1,3,0:T(8,128)(2,1)} %bitcast.191), calls=%async_computation.1 | async-start | bytes 29360128 | tf_op jit(solution)/shard_map/all_to_all | solution.py:105
  47.1 0.0 reduce-scatter.3.cloned.1.call-start
  47.2 0.0 copy-done.4
  47.2 6.5 %broadcast_select_fusion = bf16[16,7,1,128,256]{4,3,1,0,2:T(8,128)(2,1)S(1)} fusion(bf16[16,7,1,128,256]{4,3,1,0,2:T(8,128)(2,1)} %bitcast.190, pred[16,7,128]{2,1,0:T(8,128)(4,1)S(1)} %get-tuple-element.6, bf16[16,256]{1,0:T(8,128)(2,1)S(1)} %bitcast.203), kind=kLoop, calls=%fused_computation.17 | loop fusion | flops 3670016 | bytes 14702592 | tf_op jit(solution)/shard_map/jit(_where)/select_n | solution.py:60
  53.7 1.3 fusion.47
  55.0 0.2 fusion.34
  55.2 0.7 fusion.25
  55.9 8.9 %convolution_convert_fusion.1 = bf16[16,8192]{1,0:T(8,128)(2,1)} fusion(bf16[1024,8192]{1,0:T(8,128)(2,1)} %param.17, bf16[2,8,8,128]{3,2,1,0:T(8,128)(2,1)S(1)} %bitcast.201), kind=kOutput, calls=%fused_computation.10 | convolution fusion | flops 268566528 | bytes 17072128 | tf_op jit(solution)/shard_map/dot_general | solution.py:130
  64.8 0.0 reduce-scatter.3.cloned.1.call-update
  64.8 0.2 reduce-scatter.5.cloned.1.call-start
  65.1 0.0 copy-done.1
  65.1 0.3 copy.53
  65.4 0.1 bitcast_bitcast_fusion
  65.5 1.7 fusion.48
  67.2 232.4 %all-to-all-done = bf16[16,2,7,1,128,256]{5,4,2,1,3,0:T(8,128)(2,1)} async-done(((bf16[16,2,7,1,128,256]{5,4,2,1,3,0:T(8,128)(2,1)}), bf16[16,2,7,1,128,256]{5,4,2,1,3,0:T(8,128)(2,1)}, u32[]{:S(2)}, u32[]{:S(2)}) %all-to-all-start) | async-done | bytes 14680096 | tf_op jit(solution)/shard_map/all_to_all | solution.py:105
  299.6 9.1 %gather_fusion.2 = bf16[16,7,128,256]{3,2,1,0:T(8,128)(2,1)} fusion(bf16[32,7,128,256]{3,2,1,0:T(8,128)(2,1)} %bitcast.7, s32[1024]{0:T(1024)S(1)} %pad_clamp_fusion), kind=kCustom, calls=%fused_computation.2 | custom fusion | bytes 14680128 | tf_op jit(solution)/shard_map/gather | solution.py:106
  308.8 4.0 bitcast_reduce_fusion
  312.8 0.0 copy-start
  312.8 0.5 fusion.27
  313.4 0.6 fusion.16
  314.0 4.0 fusion.1
  318.0 0.0 copy-done
  318.0 8.8 %fusion.15 = bf16[16,32,1,8,128]{4,1,3,0,2:T(8,128)(2,1)S(1)} fusion(f32[16,8,32,128]{3,2,1,0:T(8,128)S(1)} %fusion.27, f32[16,7,128,32,8]{2,3,4,1,0:T(8,128)} %copy-done, f32[16,8,32]{2,1,0:T(8,128)S(1)} %max.13, pred[16,7,128]{2,1,0:T(8,128)(4,1)S(1)} %get-tuple-element.7, bf16[16,7,1,128,256]{4,3,1,0,2:T(8,128)(2,1)} %bitcast.196, ...), kind=kOutput, calls=%fused_computation.28 | convolution fusion | flops 955777024 | bytes 21542912 | tf_op jit(solution)/shard_map/chgtpr,cphrd->cthgd/dot_general | solution.py:112
  326.9 0.5 copy.39
  327.3 16.8 %convolution_convert_fusion = bf16[512,8192]{1,0:T(8,128)(2,1)} fusion(bf16[1024,8192]{1,0:T(8,128)(2,1)} %param.17, bf16[64,8,8,128]{3,2,1,0:T(8,128)(2,1)S(1)} %bitcast.198), kind=kOutput, calls=%fused_computation.7 | convolution fusion | flops 8594128896 | bytes 26214400 | tf_op jit(solution)/shard_map/dot_general | solution.py:136
  344.2 0.0 reduce-scatter.5.cloned.1.call-update
  344.2 0.0 reduce-scatter.3.cloned.1.call-done
  344.2 60.6 %reduce-scatter.5.cloned.1.call-done = bf16[512,1024]{1,0:T(8,128)(2,1)} async-done(((bf16[512,8192]{1,0:T(8,128)(2,1)}), bf16[512,1024]{1,0:T(8,128)(2,1)}) %reduce-scatter.5.cloned.1.call-update) | async-done | bytes 1048592 | tf_op jit(solution)/shard_map/reduce_scatter | solution.py:135
  (18 shorter events, 0.1 us)
Async XLA Ops:
  11.5 9.5 %copy-start.3 = (bf16[16,1,256]{2,0,1:T(8,128)(2,1)S(1)}, bf16[16,1,256]{2,0,1:T(8,128)(2,1)}, u32[]{:S(2)}) copy-start(bf16[16,1,256]{2,0,1:T(8,128)(2,1)} %param.14) | copy-start | bytes 24580
  39.0 8.2 %copy-start.4 = (bf16[16,1024]{1,0:T(8,128)(2,1)S(1)}, bf16[16,1024]{1,0:T(8,128)(2,1)}, u32[]{:S(2)}) copy-start(bf16[16,1024]{1,0:T(8,128)(2,1)} %param.13) | copy-start | bytes 98308
  39.0 260.7 %all-to-all-start = ((bf16[16,2,7,1,128,256]{5,4,2,1,3,0:T(8,128)(2,1)}), bf16[16,2,7,1,128,256]{5,4,2,1,3,0:T(8,128)(2,1)}, u32[]{:S(2)}, u32[]{:S(2)}) async-start(bf16[16,2,7,1,128,256]{5,4,2,1,3,0:T(8,128)(2,1)} %bitcast.191), calls=%async_computation.1 | async-start | bytes 29360128 | tf_op jit(solution)/shard_map/all_to_all | solution.py:105
  47.1 297.1 %reduce-scatter.3.cloned.1.call-start = ((), (), s32[]{:S(2)}) async-start(), calls=%async_computation.3 | async-start | bytes 294912 | tf_op jit(solution)/shard_map/reduce_scatter | solution.py:129
  55.9 9.2 %copy-start.1 = (bf16[512,1024]{1,0:T(8,128)(2,1)S(1)}, bf16[512,1024]{1,0:T(8,128)(2,1)}, u32[]{:S(2)}) copy-start(bf16[512,1024]{1,0:T(8,128)(2,1)} %param.15) | copy-start | bytes 3145732
  55.9 9.6 %copy-start.2 = (bf16[512,1,256]{2,0,1:T(8,128)(2,1)S(1)}, bf16[512,1,256]{2,0,1:T(8,128)(2,1)}, u32[]{:S(2)}) copy-start(bf16[512,1,256]{2,0,1:T(8,128)(2,1)} %param.16) | copy-start | bytes 786436
  64.8 339.9 %reduce-scatter.5.cloned.1.call-start = ((), (), s32[]{:S(2)}) async-start(), calls=%async_computation.4 | async-start | bytes 9437184 | tf_op jit(solution)/shard_map/reduce_scatter | solution.py:135
  312.8 5.2 %copy-start = (f32[16,7,128,32,8]{2,3,4,1,0:T(8,128)}, f32[16,7,128,32,8]{2,3,4,1,0:T(8,128)S(1)}, u32[]{:S(2)}) copy-start(f32[16,7,128,32,8]{2,3,4,1,0:T(8,128)S(1)} %get-tuple-element.11) | copy-start | bytes 44040196
Sparse Core Ops, SparseCore 0:
  65.0 33.1 reduce-scatter.2
  344.3 60.4 reduce-scatter.4
where the time goes:
time: 412 us
  waiting for transfers between devices  293 us (71%)
  matrix products  42.8 us (10%)
  local copies, waits for them, and re-layouts  31.4 us (8%)
  other arithmetic  21.7 us (5%)
  between operations  14.3 us (3%)
  starting transfers between devices  8.4 us (2%)
    all_to_all x1, waiting for transfers between devices, local(): lax.all_to_all(parcel, 'engine', split_axis=0, concat_axis=0, tiled=True)  232 us
    reduce_scatter x1, waiting for transfers between devices, local(): lax.psum_scatter(jnp.dot(tool_attn, w_out, preferred_element_type=jnp.flo...  60.6 us
    dot_general x1, matrix products, local(): jnp.dot(tool_attn, w_out, preferred_element_type=jnp.float32)  16.8 us
    select_n x2, other arithmetic, local(): jnp.where(written[:, :, None, :, None], dec_kv[:, None, :, None, :], kv_c...  13.8 us
    gather x1, local copies, waits for them, and re-layouts, local(): parcel = kv_cache[send_index]  10.5 us
    gather x1, local copies, waits for them, and re-layouts, local(): kv_cache = kv_pool[page_table]  9.43 us
    gather x1, local copies, waits for them, and re-layouts, local(): arrived = arrived.reshape((engines * CAP,) + kv_cache.shape[1:])[recv_index]  9.13 us
    dot_general x1, matrix products, local(): jnp.dot(dec_attn, w_out, preferred_element_type=jnp.float32)  8.89 us
  transfers between devices with their start and end apart: 3, of which 2 were waited for; matrix products, arithmetic and copies ran while one was open for 16% of the time, Pallas kernels for 0%

commit v1 on v0

v1 whole, which is shorter than its diff:
```python
import functools
import math

import jax
import jax.numpy as jnp
from jax import lax
from jax.experimental import pallas as pl
from jax.experimental.pallas import tpu as pltpu
from jax.sharding import PartitionSpec as P

NEG = -1e30


def plan(page_table, hist_len, new_slot, engine_id, engines):
    conv_dev = page_table.shape[0]
    half = conv_dev // 2
    slot = new_slot.reshape(engines, conv_dev)
    target = slot // conv_dev
    ids = jnp.arange(conv_dev, dtype=jnp.int32)
    before = ids[None, :] < ids[:, None]
    same = target[:, :, None] == target[:, None, :]
    rank = jnp.sum(same & before, axis=2, dtype=jnp.int32)
    doubled = jnp.sum(same, axis=2, dtype=jnp.int32) > 1
    lone_before = jnp.sum(before[None] & ~doubled[:, None, :], axis=2, dtype=jnp.int32)
    pairs = jnp.sum(doubled, axis=1, dtype=jnp.int32)[:, None] // 2
    color = jnp.where(doubled, rank, (lone_before >= half - pairs).astype(jnp.int32))
    place = jnp.sum((color[:, :, None] == color[:, None, :]) & before, axis=2, dtype=jnp.int32)
    colors = jnp.arange(2, dtype=jnp.int32)
    peers = jnp.arange(engines, dtype=jnp.int32)
    out_mask = (target == engine_id)[None] & (color[None] == colors[:, None, None])
    send = jnp.sum(jnp.where(out_mask, (slot % conv_dev)[None], 0), axis=2, dtype=jnp.int32).reshape(-1)
    home = slot[None] == (engine_id * conv_dev + ids)[:, None, None]
    final = jnp.sum(jnp.where(home, (color * engines + peers[:, None])[None], 0), axis=(1, 2), dtype=jnp.int32)
    my_target = lax.dynamic_index_in_dim(target, engine_id, 0, False)
    my_color = lax.dynamic_index_in_dim(color, engine_id, 0, False)
    my_place = lax.dynamic_index_in_dim(place, engine_id, 0, False)
    my_hist = lax.dynamic_slice_in_dim(hist_len, engine_id * conv_dev, conv_dev)
    row = my_color * half + my_place
    at = row[None, :] == ids[:, None]
    pick = lambda v: jnp.sum(jnp.where(at, v[None], 0), axis=1, dtype=jnp.int32)
    conv = pick(ids)
    parcel = pick(my_color * engines + my_target)
    hist = pick(my_hist)
    pages = jnp.sum(jnp.where(at[:, :, None], page_table[None], 0), axis=1, dtype=jnp.int32)
    back_mask = (my_target[None] == peers[:, None])[None] & (my_color[None, None] == colors[:, None, None])
    back = jnp.sum(jnp.where(back_mask, row[None, None], 0), axis=2, dtype=jnp.int32).reshape(-1)
    return dict(send=send, final=final, conv=conv, parcel=parcel, hist=hist, pages=pages, back=back, row=row)


def attend(tool_q, tool_kv, dec_q, dec_kv, pages, hist, score_scale):
    tool, head = tool_q.shape[0], dec_q.shape[1]
    group = tool_q.shape[1] // head
    page = pages[0].shape[0]
    queries = jnp.concatenate([tool_q[:, h * head : (h + 1) * head] for h in range(group)] + [dec_q], axis=0)
    rows, prefix = queries.shape[0], len(pages) * page
    fresh = jnp.concatenate(
        [tool_kv, dec_kv, jnp.zeros((page - tool - 16, 2 * head), tool_kv.dtype)],
        axis=0,
    )
    kv = jnp.concatenate(list(pages) + [fresh], axis=0)
    scores = lax.dot_general(
        queries, kv[:, :head], (((1,), (1,)), ((), ())), preferred_element_type=jnp.float32
    )
    old = jnp.where(lax.broadcasted_iota(jnp.int32, (1, prefix), 1) < hist, 0.0, NEG)
    col = lax.broadcasted_iota(jnp.int32, (rows, page), 1)
    row = lax.broadcasted_iota(jnp.int32, (rows, page), 0)
    near = ((col <= row % tool) & (row < group * tool)) | (col == tool)
    scores = jnp.concatenate(
        [scores[:, :prefix] + old, jnp.where(near, scores[:, prefix:], NEG)], axis=1
    )
    peak = jnp.max(scores, axis=1, keepdims=True)
    weights = jnp.exp2((scores - peak) * (score_scale * math.log2(math.e)))
    total = jnp.sum(weights, axis=1, keepdims=True)
    mixed = jnp.dot(weights.astype(jnp.bfloat16), kv[:, head:], preferred_element_type=jnp.float32)
    return (mixed / total).astype(jnp.bfloat16)


def attention_kernel(scale, conv_s, parcel_s, hist_s, pages_s, pool, tool_q, tool_kv, dec_q, dec_kv, out, dec_out):
    k = pl.program_id(0)
    conv, parcel = conv_s[k], parcel_s[k]
    pages = [pool[pages_s[k, p]] for p in range(pages_s.shape[1])]
    got = attend(
        tool_q[parcel], tool_kv[parcel], dec_q[conv], dec_kv[conv], pages, hist_s[k], scale
    )
    tool, head = tool_q.shape[1], dec_q.shape[2]
    group = tool_q.shape[2] // head
    for h in range(group):
        out[0, :, h * head : (h + 1) * head] = got[h * tool : (h + 1) * tool]
    dec_out[0] = got[group * tool :]


def local(kv_pool, page_table, hist_len, new_slot, dec_q, dec_kv, tool_q, tool_kv, w_out):
    engines = lax.axis_size("engine")
    engine_id = lax.axis_index("engine")
    conv_dev, pages_max = page_table.shape
    page_len, head = kv_pool.shape[2], kv_pool.shape[3] // 2
    group = dec_q.shape[1] // head
    tool = tool_q.shape[0] // conv_dev
    width = group * head
    t = plan(page_table, hist_len, new_slot, engine_id, engines)
    both = jnp.concatenate([tool_q, tool_kv[:, 0]], axis=1).reshape(conv_dev, tool, -1)
    parcels = both[t["send"]].reshape(2, engines, tool, -1)
    came = lax.all_to_all(parcels, "engine", split_axis=1, concat_axis=1, tiled=True)
    came = came.reshape(2 * engines, tool, -1)
    dec16 = jnp.pad(dec_q.reshape(conv_dev, group, head), ((0, 0), (0, 16 - group), (0, 0)))
    whole = lambda shape: pl.BlockSpec(shape, lambda k, *_: (0,) * len(shape))
    got, dec_got = pl.pallas_call(
        functools.partial(attention_kernel, head**-0.5),
        grid_spec=pltpu.PrefetchScalarGridSpec(
            num_scalar_prefetch=4,
            grid=(conv_dev,),
            in_specs=[
                whole((kv_pool.shape[0], page_len, 2 * head)),
                whole((2 * engines, tool, width)),
                whole((2 * engines, tool, 2 * head)),
                whole((conv_dev, 16, head)),
                whole((conv_dev, 16, 2 * head)),
            ],
            out_specs=[
                pl.BlockSpec((1, tool, width), lambda k, *_: (k, 0, 0)),
                pl.BlockSpec((1, 16, head), lambda k, *_: (k, 0, 0)),
            ],
        ),
        out_shape=[
            jax.ShapeDtypeStruct((conv_dev, tool, width), jnp.bfloat16),
            jax.ShapeDtypeStruct((conv_dev, 16, head), jnp.bfloat16),
        ],
        compiler_params=pltpu.CompilerParams(vmem_limit_bytes=56 * 2**20),
    )(
        t["conv"], t["parcel"], t["hist"], t["pages"],
        kv_pool[:, 0], came[..., :width], came[..., width:], dec16, jnp.broadcast_to(dec_kv, (conv_dev, 16, 2 * head)),
    )
    attn = jnp.concatenate([got.reshape(conv_dev * tool, width), dec_got[:, :group].reshape(conv_dev, width)])
    sums = lax.psum_scatter(
        jnp.dot(attn, w_out, preferred_element_type=jnp.float32).astype(jnp.bfloat16),
        "tp", scatter_dimension=1, tiled=True,
    )
    rows = sums[: conv_dev * tool].reshape(conv_dev, tool, -1)
    dec_out = sums[conv_dev * tool :][t["row"]]
    back = rows[t["back"]].reshape(2, engines, tool, -1)
    home = lax.all_to_all(back, "engine", split_axis=1, concat_axis=1, tiled=True)
    tool_out = home.reshape(2 * engines, tool, -1)[t["final"]].reshape(conv_dev * tool, -1)
    return dec_out, tool_out


def solution(mesh):
    return jax.shard_map(
        local,
        mesh=mesh,
        in_specs=(
            P("engine", "tp", None, None),
            P("engine", None),
            P(),
            P(),
            P("engine", "tp"),
            P("engine", "tp", None),
            P("engine", "tp"),
            P("engine", "tp", None),
            P("tp", None),
        ),
        out_specs=(P("engine", "tp"), P("engine", "tp")),
        check_vma=False,
    )
```

time: 412 us -> 206 us (0.50)
  waiting for transfers between devices: 293 us -> 114 us
  matrix products: 42.8 us -> 15 us
  Pallas kernels: 0 us -> 20.5 us
  other arithmetic: 21.7 us -> 4.85 us
  local copies, waits for them, and re-layouts: 31.4 us -> 21.6 us
  starting transfers between devices: 8.4 us -> 15.2 us
    all_to_all x1 -> x2, waiting for transfers between devices: 232 us -> 61.7 us  [the longest x1 34.2 us: local(): lax.all_to_all(parcels, 'engine', split_axis=1, concat_axis=1, tiled=True)]
    dot_general x8 -> x1, matrix products: 42.8 us -> 15 us  [local(): jnp.dot(attn, w_out, preferred_element_type=jnp.float32)]
    gather x3 -> x4, local copies, waits for them, and re-layouts: 29.1 us -> 7.3 us  [the longest x1 3.17 us: local(): home.reshape(2 * engines, tool, -1)[t['final']].reshape(conv_dev * tool, -1)]
    pallas_call x0 -> x1, Pallas kernels: none -> 20.5 us  [local(): pl.pallas_call(functools.partial(attention_kernel, head ** (-0.5)), grid_...]
    select_n x6 -> x5, other arithmetic: 15.2 us -> 0.05 us  [the longest x1 0.02 us: local(): dec_out = sums[conv_dev * tool:][t['row']]]
    reduce_scatter x2 -> x1, waiting for transfers between devices: 60.6 us -> 52.3 us  [local(): lax.psum_scatter(jnp.dot(attn, w_out, preferred_element_type=jnp.float32)...]
    all_to_all x1 -> x2, starting transfers between devices: 8.14 us -> 15.2 us  [the longest x1 8.09 us: local(): lax.all_to_all(parcels, 'engine', split_axis=1, concat_axis=1, tiled=True)]
    reshape x1 -> x5, local copies, waits for them, and re-layouts: 0.08 us -> 5.96 us  [the longest x1 3.47 us: local(): parcels = both[t['send']].reshape(2, engines, tool, -1)]
  transfers between devices with their start and end apart: 3 -> 3, of which waited for: 2 -> 3; matrix products, arithmetic and copies ran while one was open for 16% -> 2% of each run, Pallas kernels for 0% -> 0%
where the time goes in v1:
time: 206 us; the launch traced here: 205 us
  waiting for transfers between devices  114 us (55%)
  local copies, waits for them, and re-layouts  21.6 us (10%)
  Pallas kernels  20.5 us (10%)
  starting transfers between devices  15.2 us (7%)
  matrix products  15 us (7%)
  between operations  14.2 us (7%)
  other arithmetic  4.85 us (2%)
    reduce_scatter x1, waiting for transfers between devices, local(): lax.psum_scatter(jnp.dot(attn, w_out, preferred_element_type=jnp.float32)...  52.3 us
    all_to_all x1, waiting for transfers between devices, local(): lax.all_to_all(parcels, 'engine', split_axis=1, concat_axis=1, tiled=True)  34.2 us
    all_to_all x1, waiting for transfers between devices, local(): lax.all_to_all(back, 'engine', split_axis=1, concat_axis=1, tiled=True)  27.5 us
    pallas_call x1, Pallas kernels, local(): pl.pallas_call(functools.partial(attention_kernel, head ** (-0.5)), grid_...  20.5 us
    dot_general x1, matrix products, local(): jnp.dot(attn, w_out, preferred_element_type=jnp.float32)  15 us
    all_to_all x1, starting transfers between devices, local(): lax.all_to_all(parcels, 'engine', split_axis=1, concat_axis=1, tiled=True)  8.09 us
    all_to_all x1, starting transfers between devices, local(): lax.all_to_all(back, 'engine', split_axis=1, concat_axis=1, tiled=True)  7.08 us
  transfers between devices with their start and end apart: 3, of which 3 were waited for; matrix products, arithmetic and copies ran while one was open for 2% of the time, Pallas kernels for 0%

profile of v1, /device:TPU:0, one launch (start us, length us, event | category | flops | bytes accessed | tf_op | source)
XLA Modules:
  0.0 205.3 jit_solution(17601661942421804265)
XLA Ops:
  7.2 0.8 reshape.476
  8.0 0.7 convert_reduce_fusion.2
  8.7 0.1 convert_reduce_fusion.3
  8.8 0.4 convert_reduce_fusion.1
  9.2 0.1 iota_add_fusion
  9.2 0.1 select_reduce_fusion.3
  9.4 0.1 reshape.477
  9.5 1.4 pad_maximum_fusion
  10.9 2.2 %gather_fusion = bf16[32,32,1280]{2,1,0:T(8,128)(2,1)} fusion(bf16[16,32,1280]{2,1,0:T(8,128)(2,1)S(1)} %pad_maximum_fusion, s32[1024]{0:T(1024)S(1)} %pad_clamp_fusion.3), kind=kCustom, calls=%fused_computation | custom fusion | bytes 5243008 | tf_op jit(solution)/shard_map/gather | solution.py:102
  13.1 3.5 %copy.19 = bf16[2,16,32,1280]{3,2,0,1:T(8,128)(2,1)} copy(bf16[2,16,32,1280]{3,2,1,0:T(8,128)(2,1)} %bitcast.40) | data formatting | bytes 5242880 | tf_op jit(solution)/shard_map/reshape | solution.py:102
  16.6 0.0 copy-start.2
  16.6 0.0 copy-start
  16.6 0.0 copy-start.3
  16.6 8.1 %all-to-all-start = ((bf16[2,16,32,1280]{3,2,0,1:T(8,128)(2,1)}), bf16[2,16,32,1280]{3,2,0,1:T(8,128)(2,1)S(1)}, u32[]{:S(2)}, u32[]{:S(2)}) async-start(bf16[2,16,32,1280]{3,2,0,1:T(8,128)(2,1)} %copy.19), calls=%async_computation | async-start | bytes 5242880 | tf_op jit(solution)/shard_map/all_to_all | solution.py:103
  24.7 0.0 reduce-scatter.2.cloned.1.call-start
  24.8 0.4 convert_reduce_fusion
  25.2 0.0 copy-done.2
  25.2 0.2 select_reduce_fusion.1
  25.4 0.7 copy.21.pages_s
  26.1 0.0 copy-done
  26.1 0.0 copy-done.3
  26.2 0.1 dynamic_slice.18
  26.2 0.6 pad.4.dec_q
  26.9 0.7 select_reduce_fusion.4
  27.6 34.2 %all-to-all-done = bf16[2,16,32,1280]{3,2,0,1:T(8,128)(2,1)S(1)} async-done(((bf16[2,16,32,1280]{3,2,0,1:T(8,128)(2,1)}), bf16[2,16,32,1280]{3,2,0,1:T(8,128)(2,1)S(1)}, u32[]{:S(2)}, u32[]{:S(2)}) %all-to-all-start) | async-done | bytes 2621472 | tf_op jit(solution)/shard_map/all_to_all | solution.py:103
  61.8 0.2 copy.20
  62.0 0.8 slice.29.tool_kv
  62.8 0.0 copy-start.1
  62.8 1.6 slice.28.tool_q
  64.5 0.0 copy-done.1
  64.5 0.7 broadcast_in_dim.127.dec_kv
  65.1 20.5 %shard_map.104 = (bf16[16,32,1024]{2,1,0:T(8,128)(2,1)}, bf16[16,16,128]{2,1,0:T(8,128)(2,1)}) custom-call(s32[16]{0:T(128)} %get-tuple-element.10.conv_s, s32[16]{0:T(128)} %get-tuple-element.9.parcel_s, s32[16]{0:T(128)} %get-tuple-element.8.hist_s, s32[16,7]{1,0:T(8,128)} %copy.21.pages_s, bf16[112,128,256]{2,1,0:T(8,128)(2,1)} %bitcast.45, ...), custom_call_target="tpu_custom_call" | custom-call | tf_op jit(solution)/shard_map/pallas_call | solution.py:107
  85.6 0.8 slice.17
  86.3 15.0 %convolution_convert_fusion = bf16[528,8192]{1,0:T(8,128)(2,1)} fusion(bf16[1024,8192]{1,0:T(8,128)(2,1)} %param.17, bf16[16,1024]{1,0:T(8,128)(2,1)S(1)} %bitcast.53, bf16[512,1024]{1,0:T(8,128)(2,1)} %bitcast.57), kind=kOutput, calls=%fused_computation.4 | convolution fusion | flops 8864858112 | bytes 26509312 | tf_op jit(solution)/shard_map/dot_general | solution.py:135
  101.3 0.0 reduce-scatter.2.cloned.1.call-update
  101.4 0.1 select_reduce_fusion.2
  101.5 0.1 reshape.484
  101.6 52.3 %reduce-scatter.2.cloned.1.call-done = bf16[528,1024]{1,0:T(8,128)(2,1)} async-done(((bf16[528,8192]{1,0:T(8,128)(2,1)}), bf16[528,1024]{1,0:T(8,128)(2,1)}) %reduce-scatter.2.cloned.1.call-update) | async-done | bytes 1081360 | tf_op jit(solution)/shard_map/reduce_scatter | solution.py:134
  153.9 1.2 slice-done
  155.2 0.7 gather_fusion.2
  155.9 1.6 copy.22
  157.4 7.1 %all-to-all-start.1 = ((bf16[2,16,32,1024]{3,2,0,1:T(8,128)(2,1)}), bf16[2,16,32,1024]{3,2,0,1:T(8,128)(2,1)S(1)}, u32[]{:S(2)}, u32[]{:S(2)}) async-start(bf16[2,16,32,1024]{3,2,0,1:T(8,128)(2,1)} %copy.22), calls=%async_computation.2 | async-start | bytes 4194304 | tf_op jit(solution)/shard_map/all_to_all | solution.py:141
  164.5 0.4 select_reduce_fusion
  165.0 0.0 slice-done.1
  165.0 1.2 gather_fusion.1
  166.2 27.5 %all-to-all-done.1 = bf16[2,16,32,1024]{3,2,0,1:T(8,128)(2,1)S(1)} async-done(((bf16[2,16,32,1024]{3,2,0,1:T(8,128)(2,1)}), bf16[2,16,32,1024]{3,2,0,1:T(8,128)(2,1)S(1)}, u32[]{:S(2)}, u32[]{:S(2)}) %all-to-all-start.1) | async-done | bytes 2097184 | tf_op jit(solution)/shard_map/all_to_all | solution.py:141
  193.7 1.6 copy.23
  195.3 3.2 %gather_fusion.3 = bf16[16,32,1024]{2,1,0:T(8,128)(2,1)} fusion(bf16[32,32,1024]{2,1,0:T(8,128)(2,1)} %bitcast.46, s32[1024]{0:T(1024)S(1)} %pad_clamp_fusion), kind=kCustom, calls=%fused_computation.3 | custom fusion | bytes 2097216 | tf_op jit(solution)/shard_map/gather | solution.py:142
  (22 shorter events, 0.2 us)
Async XLA Ops:
  16.6 8.6 %copy-start.2 = (s32[16,7]{0,1:T(8,128)S(1)}, s32[16,7]{0,1:T(8,128)}, u32[]{:S(2)}) copy-start(s32[16,7]{0,1:T(8,128)} %param.10) | copy-start | bytes 1348
  16.6 9.5 %copy-start = (bf16[16,1024]{1,0:T(8,128)(2,1)S(1)}, bf16[16,1024]{1,0:T(8,128)(2,1)}, u32[]{:S(2)}) copy-start(bf16[16,1024]{1,0:T(8,128)(2,1)} %param.13) | copy-start | bytes 98308
  16.6 9.5 %copy-start.3 = (s32[256]{0:T(256)S(1)}, s32[256]{0:T(256)}, u32[]{:S(2)}) copy-start(s32[256]{0:T(256)} %param.11) | copy-start | bytes 3076
  16.6 45.2 %all-to-all-start = ((bf16[2,16,32,1280]{3,2,0,1:T(8,128)(2,1)}), bf16[2,16,32,1280]{3,2,0,1:T(8,128)(2,1)S(1)}, u32[]{:S(2)}, u32[]{:S(2)}) async-start(bf16[2,16,32,1280]{3,2,0,1:T(8,128)(2,1)} %copy.19), calls=%async_computation | async-start | bytes 5242880 | tf_op jit(solution)/shard_map/all_to_all | solution.py:103
  24.7 129.2 %reduce-scatter.2.cloned.1.call-start = ((), (), s32[]{:S(2)}) async-start(), calls=%async_computation.3 | async-start | bytes 9732096 | tf_op jit(solution)/shard_map/reduce_scatter | solution.py:134
  62.8 1.7 copy-start.1
  153.9 1.2 slice-start
  157.4 7.6 %slice-start.1 = ((bf16[528,1024]{1,0:T(8,128)(2,1)}), bf16[16,1024]{1,0:T(8,128)(2,1)S(1)}, s32[]{:S(2)}) async-start(bf16[528,1024]{1,0:T(8,128)(2,1)} %reduce-scatter.2.cloned.1.call-done), calls=%async_computation.5 | async-start | bytes 65536 | tf_op jit(solution)/shard_map/slice | solution.py:139
  157.4 36.3 %all-to-all-start.1 = ((bf16[2,16,32,1024]{3,2,0,1:T(8,128)(2,1)}), bf16[2,16,32,1024]{3,2,0,1:T(8,128)(2,1)S(1)}, u32[]{:S(2)}, u32[]{:S(2)}) async-start(bf16[2,16,32,1024]{3,2,0,1:T(8,128)(2,1)} %copy.22), calls=%async_computation.2 | async-start | bytes 4194304 | tf_op jit(solution)/shard_map/all_to_all | solution.py:141
Sparse Core Ops, SparseCore 0:
  101.5 52.4 reduce-scatter.1

commit v2 on v1

v2 whole, which is shorter than its diff:
```python
import functools
import math

import jax
import jax.numpy as jnp
from jax import lax
from jax.experimental import pallas as pl
from jax.experimental.pallas import tpu as pltpu
from jax.sharding import PartitionSpec as P

NEG = -1e30
MESH = pl.DeviceIdType.MESH
BF16, F32 = jnp.bfloat16, jnp.float32
COLORS = 2
CUTS = 2
CHIPS = 4


def plan(page_table, hist_len, new_slot, engine_id, engines):
    conv_dev = page_table.shape[0]
    half = conv_dev // 2
    slot = new_slot.reshape(engines, conv_dev)
    target = slot // conv_dev
    ids = jnp.arange(conv_dev, dtype=jnp.int32)
    before = ids[None, :] < ids[:, None]
    same = target[:, :, None] == target[:, None, :]
    rank = jnp.sum(same & before, axis=2, dtype=jnp.int32)
    doubled = jnp.sum(same, axis=2, dtype=jnp.int32) > 1
    lone_before = jnp.sum(before[None] & ~doubled[:, None, :], axis=2, dtype=jnp.int32)
    pairs = jnp.sum(doubled, axis=1, dtype=jnp.int32)[:, None] // 2
    color = jnp.where(doubled, rank, (lone_before >= half - pairs).astype(jnp.int32))
    place = jnp.sum((color[:, :, None] == color[:, None, :]) & before, axis=2, dtype=jnp.int32)
    colors = jnp.arange(2, dtype=jnp.int32)
    peers = jnp.arange(engines, dtype=jnp.int32)
    out_mask = (target == engine_id)[None] & (color[None] == colors[:, None, None])
    send = jnp.sum(jnp.where(out_mask, (slot % conv_dev)[None], 0), axis=2, dtype=jnp.int32).reshape(-1)
    home = slot[None] == (engine_id * conv_dev + ids)[:, None, None]
    final = jnp.sum(jnp.where(home, (color * engines + peers[:, None])[None], 0), axis=(1, 2), dtype=jnp.int32)
    my_target = lax.dynamic_index_in_dim(target, engine_id, 0, False)
    my_color = lax.dynamic_index_in_dim(color, engine_id, 0, False)
    my_place = lax.dynamic_index_in_dim(place, engine_id, 0, False)
    my_hist = lax.dynamic_slice_in_dim(hist_len, engine_id * conv_dev, conv_dev)
    row = my_color * half + my_place
    at = row[None, :] == ids[:, None]
    pick = lambda v: jnp.sum(jnp.where(at, v[None], 0), axis=1, dtype=jnp.int32)
    pages = jnp.sum(jnp.where(at[:, :, None], page_table[None], 0), axis=1, dtype=jnp.int32)
    back_mask = (my_target[None] == peers[:, None])[None] & (my_color[None, None] == colors[:, None, None])
    back = jnp.sum(jnp.where(back_mask, my_place[None, None], 0), axis=2, dtype=jnp.int32).reshape(-1)
    return jnp.concatenate(
        [send, back, final, pick(ids), pick(my_target), my_hist, pick(my_hist)]
        + [page_table.reshape(-1), pages.reshape(-1)]
    ).astype(jnp.int32)


def attend(queries, pages, fresh, bias, near, scale):
    head = queries.shape[1]
    kv = jnp.concatenate(list(pages) + [fresh], axis=0)
    prefix = bias.shape[1]
    scores = lax.dot_general(queries, kv[:, :head], (((1,), (1,)), ((), ())), preferred_element_type=F32)
    near = jnp.concatenate([near] * (queries.shape[0] // near.shape[0]), axis=0)
    scores = jnp.concatenate([scores[:, :prefix] + bias, scores[:, prefix:] + near], axis=1)
    peak = jnp.max(scores, axis=1, keepdims=True)
    weights = jnp.exp2((scores - peak) * (scale * math.log2(math.e)))
    total = jnp.sum(weights, axis=1, keepdims=True)
    mixed = jnp.dot(weights.astype(BF16), kv[:, head:], preferred_element_type=F32)
    return mixed / total


def kernel(
    tab, pool_hbm, w_hbm, tool_q, tool_kv, dec_q, dec_kv, out, dec_out,
    pool, w, fsend, frecv_0, frecv_1, frecv_2, frecv_3, attn0, attn, heads, part0, part, got0, got, sums0, sums,
    two0, two, direct0, direct, rows0, rows, bsend, brecv,
    pool_sem, w_sem, fs, fr, xs, xr, ys, yr, bs, br,
    *, engines, conv_dev, pages_max,
):
    stages = COLORS * CUTS
    frecv = [frecv_0, frecv_1, frecv_2, frecv_3]
    half = conv_dev // COLORS
    cut = tool_q.shape[2]
    head = dec_q.shape[2]
    width = tool_q.shape[3]
    group = width // head
    page = pool.shape[1]
    prefix = pages_max * page
    scale = head**-0.5
    width_out = w.shape[2]
    side = width_out // 2
    main = half * cut
    SEND, BACK = 0, COLORS * engines
    FINAL = BACK + COLORS * engines
    CONV = FINAL + conv_dev
    DEST = CONV + conv_dev
    HIST = DEST + conv_dev
    PAGES = HIST + 2 * conv_dev

    me, tp = lax.axis_index("engine"), lax.axis_index("tp")
    y, core = tp // 2, tp % 2
    partner = (me, y * 2 + 1 - core)
    up = (me, (y + 1) % CHIPS * 2 + core)
    down = (me, (y + CHIPS - 1) % CHIPS * 2 + core)
    other = lambda k: lax.rem(me + k, engines)

    barrier = pltpu.get_barrier_semaphore()

    @pl.loop(1, engines)
    def _(k):
        pl.semaphore_signal(barrier, inc=1, device_id=(other(k), tp), device_id_type=MESH)

    for peer in (partner, up, down):
        pl.semaphore_signal(barrier, inc=1, device_id=peer, device_id_type=MESH)

    load_pool = pltpu.make_async_copy(pool_hbm, pool, pool_sem)
    load_pool.start()
    load_w = [
        pltpu.make_async_copy(w_hbm.at[:, pl.ds(b * width_out, width_out)], w.at[b], w_sem.at[b])
        for b in range(2 * CHIPS)
    ]

    def fill(ref, s, engine):
        slot = tab[SEND + s // CUTS * engines + engine]
        ref[engine, :, :width] = tool_q[slot, s % CUTS]
        ref[engine, :, width:] = tool_kv[slot, s % CUTS]

    def fwd(s, k):
        return pltpu.make_async_remote_copy(
            fsend.at[s, other(k)], frecv[s].at[me], fs.at[s, other(k)], fr.at[s, me],
            device_id=(other(k), tp), device_id_type=MESH,
        )

    def fwd_in(s, k):
        return pltpu.make_async_remote_copy(
            fsend.at[s, me], frecv[s].at[other(k)], fs.at[s, me], fr.at[s, other(k)],
            device_id=(other(k), tp), device_id_type=MESH,
        )

    for s in range(stages):

        @pl.loop(1, engines)
        def _(k, s=s):
            fill(fsend.at[s], s, other(k))

        if s == 0:
            pl.semaphore_wait(barrier, engines - 1 + 3)

        @pl.loop(1, engines)
        def _(k, s=s):
            fwd(s, k).start()

        fill(frecv[s], s, me)
    for copy in load_w:
        copy.start()

    def pages_of(row):
        return [pool[tab[PAGES + row * pages_max + p]] for p in range(pages_max)]

    def bias_of(row):
        return jnp.where(lax.broadcasted_iota(jnp.int32, (1, prefix), 1) < tab[HIST + row], 0.0, NEG)

    col = lax.broadcasted_iota(jnp.int32, (16, page), 1)
    row = lax.broadcasted_iota(jnp.int32, (16, page), 0)

    load_pool.wait()
    only = jnp.where(col == 0, 0.0, NEG)

    @pl.loop(0, conv_dev)
    def _(i):
        fresh = jnp.concatenate([dec_kv[i], jnp.zeros((page - 16, 2 * head), BF16)], axis=0)
        got_i = attend(dec_q[i], pages_of(i), fresh, bias_of(i), only, scale)
        for h in range(group):
            heads[h, pl.ds(i, 1), :] = got_i[h : h + 1]

    for h in range(group):
        attn0[main:, h * head : (h + 1) * head] = heads[h].astype(BF16)

    def of(first, later, s):
        return first if s == 0 else later.at[s - 1]

    def attention(s):
        color, u = s // CUTS, s % CUTS

        @pl.loop(1, engines)
        def _(k):
            fwd_in(s, k).wait_recv()

        known = (u + 1) * cut
        near = jnp.where(((col <= row + u * cut) & (col < known)) | (col == known), 0.0, NEG)
        dst = of(attn0, attn, s)

        @pl.loop(0, half)
        def _(j):
            conv = tab[CONV + color * half + j]
            at = conv_dev + color * half + j
            dest = tab[DEST + color * half + j]
            kv_new = [frecv[color * CUTS + v][dest, :, width:] for v in range(u + 1)]
            fresh = jnp.concatenate(
                kv_new + [dec_kv[conv], jnp.zeros((page - 16 - known, 2 * head), BF16)], axis=0
            )
            q = frecv[s][dest, :, :width]
            queries = jnp.concatenate([q[:, h * head : (h + 1) * head] for h in range(group)], axis=0)
            got_j = attend(queries, pages_of(at), fresh, bias_of(at), near, scale).astype(BF16)
            for h in range(group):
                dst[pl.ds(pl.multiple_of(j * cut, cut), cut), h * head : (h + 1) * head] = got_j[
                    h * cut : (h + 1) * cut
                ]

    def swap(s, k):
        return pltpu.make_async_remote_copy(
            of(part0, part, s).at[2 * k], of(got0, got, s).at[k], xs.at[s, k], xr.at[s, k],
            device_id=partner, device_id_type=MESH,
        )

    def hop(s, n, src, dst, to):
        return pltpu.make_async_remote_copy(src, dst, ys.at[s, n], yr.at[s, n], device_id=to, device_id_type=MESH)

    def ring(s):
        a, t, d = of(sums0, sums, s), of(two0, two, s), of(direct0, direct, s)
        return [
            hop(s, 0, a.at[0, 0], t.at[0], up),
            hop(s, 1, a.at[0, 1], t.at[1], down),
            hop(s, 2, a.at[1, 1], d.at[0, 1], up),
            hop(s, 3, a.at[2, 0], d.at[1, 0], down),
            hop(s, 4, a.at[1, 0], d.at[0, 0], up),
            hop(s, 5, a.at[2, 1], d.at[1, 1], down),
        ]

    def finish(s, k):
        swap(s, k).wait_recv()
        mine, came, a = of(part0, part, s), of(got0, got, s), of(sums0, sums, s)
        for v in range(2):
            cols = slice(v * side, (v + 1) * side)
            a[k, v] = (mine[2 * k + 1, :, cols].astype(F32) + came[k, :, cols].astype(F32)).astype(BF16)

    def project(s):
        src, dst = of(attn0, attn, s), of(part0, part, s)
        steps = ring(s)

        @pl.loop(0, 2 * CHIPS)
        def _(b):
            k = b // 2
            far = lax.rem(2 - k - k // 2 + 2 * (k // 3) + y + CHIPS, CHIPS)
            block = far * 2 + lax.rem(core + 1 + b % 2, 2)
            dst[b] = jnp.dot(src[...], w[block], preferred_element_type=F32).astype(BF16)

            @pl.when(b % 2 == 0)
            def _():
                swap(s, k).start()

            @pl.when((b % 2 == 1) & (b > 1))
            def _():
                finish(s, k - 1)

            @pl.when(b == 3)
            def _():
                steps[0].start()
                steps[1].start()

            @pl.when(b == 5)
            def _():
                steps[2].start()

            @pl.when(b == 7)
            def _():
                steps[3].start()

        finish(s, CHIPS - 1)

    def relay(s):
        a, t, steps = of(sums0, sums, s), of(two0, two, s), ring(s)
        for v, k in ((0, 1), (1, 2)):
            steps[v].wait_recv()
            a[k, v] = (a[k, v].astype(F32) + t[v].astype(F32)).astype(BF16)
            steps[4 + v].start()

    def back(s, k):
        color, u = s // CUTS, s % CUTS
        return pltpu.make_async_remote_copy(
            bsend.at[s, other(k)], brecv.at[u, color * engines + me], bs.at[s, other(k)], br.at[s, me],
            device_id=(other(k), tp), device_id_type=MESH,
        )

    def back_in(s, k):
        color, u = s // CUTS, s % CUTS
        return pltpu.make_async_remote_copy(
            bsend.at[s, me], brecv.at[u, color * engines + other(k)], bs.at[s, me], br.at[s, other(k)],
            device_id=(other(k), tp), device_id_type=MESH,
        )

    def deliver(s):
        color, u = s // CUTS, s % CUTS
        a, d, dst = of(sums0, sums, s), of(direct0, direct, s), of(rows0, rows, s)
        steps = ring(s)
        for n in range(2, 6):
            steps[n].wait_recv()
        for v in range(2):
            total = (a[3, v].astype(F32) + d[0, v].astype(F32) + d[1, v].astype(F32)).astype(BF16)
            dst[:, :, v * side : (v + 1) * side] = total.reshape(-1, cut, side)

        def mine(engine):
            place = tab[BACK + color * engines + engine]
            return dst[place]

        @pl.loop(1, engines)
        def _(k):
            bsend[s, other(k)] = mine(other(k))
            back(s, k).start()

        brecv[u, color * engines + me] = mine(me)
        if s == 0:
            dec_out[...] = dst[half]

    for s in range(stages):
        attention(s)
        if s == 0:
            for copy in load_w:
                copy.wait()
        else:
            relay(s - 1)
        project(s)
        if s > 0:
            deliver(s - 1)
    relay(stages - 1)
    deliver(stages - 1)

    for s in range(stages):

        @pl.loop(1, engines)
        def _(k, s=s):
            back_in(s, k).wait_recv()

    @pl.loop(0, conv_dev)
    def _(n):
        for u in range(CUTS):
            out[n, u] = brecv[u, tab[FINAL + n]]

    for s in range(stages):

        @pl.loop(1, engines)
        def _(k, s=s):
            fwd(s, k).wait_send()
            back(s, k).wait_send()

        for k in range(CHIPS):
            swap(s, k).wait_send()
        for step in ring(s):
            step.wait_send()


def local(kv_pool, page_table, hist_len, new_slot, dec_q, dec_kv, tool_q, tool_kv, w_out):
    engines = lax.axis_size("engine")
    conv_dev, pages_max = page_table.shape
    page, head = kv_pool.shape[2], kv_pool.shape[3] // 2
    width = dec_q.shape[1]
    group = width // head
    tool_rows = tool_q.shape[0]
    cut = tool_rows // conv_dev // CUTS
    width_out = w_out.shape[1] // (2 * CHIPS)
    side = width_out // 2
    stages = COLORS * CUTS
    main = conv_dev // COLORS * cut
    tab = plan(page_table, hist_len, new_slot, lax.axis_index("engine"), engines)
    dec16 = jnp.pad(dec_q.reshape(conv_dev, group, head), ((0, 0), (0, 16 - group), (0, 0)))
    kv16 = jnp.broadcast_to(dec_kv, (conv_dev, 16, 2 * head))
    vmem = lambda shape: pltpu.VMEM(shape, BF16)
    split = lambda lead, cols: [
        vmem(lead + (main + conv_dev, cols)),
        vmem((stages - 1,) + lead + (main, cols)),
    ]
    dma = pltpu.SemaphoreType.DMA
    in_vmem = pl.BlockSpec(memory_space=pltpu.VMEM)
    anywhere = pl.BlockSpec(memory_space=pl.ANY)
    tool_out, dec_out = pl.pallas_call(
        functools.partial(kernel, engines=engines, conv_dev=conv_dev, pages_max=pages_max),
        out_shape=[
            jax.ShapeDtypeStruct((conv_dev, CUTS, cut, width_out), BF16),
            jax.ShapeDtypeStruct((conv_dev, width_out), BF16),
        ],
        in_specs=[pl.BlockSpec(memory_space=pltpu.SMEM), anywhere, anywhere] + [in_vmem] * 4,
        out_specs=[in_vmem, in_vmem],
        scratch_shapes=[
            vmem((kv_pool.shape[0], page, 2 * head)),
            vmem((2 * CHIPS, w_out.shape[0], width_out)),
            vmem((stages, engines, cut, width + 2 * head)),
            *[vmem((engines, cut, width + 2 * head)) for _ in range(stages)],
            *split((), width),
            pltpu.VMEM((group, conv_dev, head), F32),
            *split((2 * CHIPS,), width_out),
            *split((CHIPS,), width_out),
            *split((CHIPS, 2), side),
            *split((2,), side),
            *split((2, 2), side),
            vmem((conv_dev // COLORS + 1, cut, width_out)),
            vmem((stages - 1, conv_dev // COLORS, cut, width_out)),
            vmem((stages, engines, cut, width_out)),
            vmem((CUTS, COLORS * engines, cut, width_out)),
            dma(()),
            dma((2 * CHIPS,)),
            dma((stages, engines)),
            dma((stages, engines)),
            dma((stages, CHIPS)),
            dma((stages, CHIPS)),
            dma((stages, 6)),
            dma((stages, 6)),
            dma((stages, engines)),
            dma((stages, engines)),
        ],
        compiler_params=pltpu.CompilerParams(
            collective_id=0, has_side_effects=True, vmem_limit_bytes=62 * 2**20
        ),
        cost_estimate=pl.CostEstimate(
            flops=2 * (tool_rows + conv_dev) * w_out.size, bytes_accessed=2 * (w_out.size + kv_pool.size), transcendentals=0
        ),
    )(
        tab, kv_pool[:, 0], w_out, tool_q.reshape(conv_dev, CUTS, cut, width),
        tool_kv.reshape(conv_dev, CUTS, cut, 2 * head), dec16, kv16,
    )
    return dec_out, tool_out.reshape(tool_rows, width_out)


def solution(mesh):
    return jax.shard_map(
        local,
        mesh=mesh,
        in_specs=(
            P("engine", "tp", None, None),
            P("engine", None),
            P(),
            P(),
            P("engine", "tp"),
            P("engine", "tp", None),
            P("engine", "tp"),
            P("engine", "tp", None),
            P("tp", None),
        ),
        out_specs=(P("engine", "tp"), P("engine", "tp")),
        check_vma=False,
    )
```

time: 206 us -> 99.5 us (0.48)
  waiting for transfers between devices: 114 us -> 0 us
  Pallas kernels: 20.5 us -> 85.1 us
  starting transfers between devices: 15.2 us -> 0 us
  matrix products: 15 us -> 0 us
  between operations: 14.2 us -> 0.73 us
  local copies, waits for them, and re-layouts: 21.6 us -> 9.78 us
    pallas_call x1, Pallas kernels: 20.5 us -> 85.1 us  [local(): pl.pallas_call(functools.partial(kernel, engines=engines, conv_dev=conv_d...]
    all_to_all x2 -> x0, waiting for transfers between devices: 61.7 us -> none  [the longest x1 34.2 us: local(): lax.all_to_all(parcels, 'engine', split_axis=1, concat_axis=1, tiled=True)]
    reduce_scatter x1 -> x0, waiting for transfers between devices: 52.3 us -> none  [local(): lax.psum_scatter(jnp.dot(attn, w_out, preferred_element_type=jnp.float32)...]
    all_to_all x2 -> x0, starting transfers between devices: 15.2 us -> none  [the longest x1 8.09 us: local(): lax.all_to_all(parcels, 'engine', split_axis=1, concat_axis=1, tiled=True)]
    dot_general x1 -> x0, matrix products: 15 us -> none  [local(): jnp.dot(attn, w_out, preferred_element_type=jnp.float32)]
    gather x4 -> x0, local copies, waits for them, and re-layouts: 7.3 us -> none  [the longest x1 3.17 us: local(): home.reshape(2 * engines, tool, -1)[t['final']].reshape(conv_dev * tool, -1)]
    unnamed x10 -> x4, local copies, waits for them, and re-layouts: 0.03 us -> 5.17 us
    reshape x3, local copies, waits for them, and re-layouts: 5.12 us -> 0.26 us  [the longest x1 0.09 us: plan(): pages.reshape(-1)]
  transfers between devices with their start and end apart: 3 -> 0, of which waited for: 3 -> 0; matrix products, arithmetic and copies ran while one was open for 2% -> 0% of each run, Pallas kernels for 0% -> 0%
where the time goes in v2:
time: 99.5 us; the launch traced here: 99.1 us
  Pallas kernels  85.1 us (86%)
  local copies, waits for them, and re-layouts  9.78 us (10%)
  other arithmetic  3.48 us (3%)
    pallas_call x1, Pallas kernels, local(): pl.pallas_call(functools.partial(kernel, engines=engines, conv_dev=conv_d...  85.1 us
    unnamed x4, local copies, waits for them, and re-layouts  5.17 us

profile of v2, /device:TPU:0, one launch (start us, length us, event | category | flops | bytes accessed | tf_op | source)
XLA Modules:
  0.0 99.1 jit_solution(7948612700508782423)
XLA Ops:
  0.6 0.8 dynamic_slice.19
  1.4 0.8 reshape.354
  2.2 0.8 copy.15
  2.9 0.1 reshape.357
  3.1 0.7 convert_reduce_fusion.2
  3.8 0.1 convert_reduce_fusion.3
  3.9 0.4 convert_reduce_fusion.1
  4.3 0.1 iota_add_fusion
  4.4 0.1 select_reduce_fusion.3
  4.5 0.1 reshape.355
  4.6 0.4 select_reduce_fusion
  5.0 0.4 convert_reduce_fusion
  5.5 0.1 select_reduce_fusion.2
  5.6 0.1 reshape.356
  5.7 0.1 select_reduce_fusion.4
  5.8 0.9 select_reduce_fusion.1
  6.7 0.1 copy.16
  6.8 0.1 reshape.358
  6.9 0.7 concatenate.3.tab
  7.6 0.8 copy.17
  8.4 0.6 pad.4.dec_q
  9.0 1.4 %broadcast_in_dim.123.dec_kv = bf16[16,16,256]{2,1,0:T(8,128)(2,1)} broadcast(bf16[16,256]{1,0:T(8,128)(2,1)} %bitcast.18), dimensions={0,2} | broadcast | bytes 139264 | tf_op jit(solution)/shard_map/broadcast_in_dim | solution.py:362
  10.4 85.1 %shard_map.104 = (bf16[16,2,16,1024]{3,2,1,0:T(8,128)(2,1)}, bf16[16,1024]{1,0:T(8,128)(2,1)}) custom-call(s32[368]{0:T(512)} %concatenate.3.tab, bf16[112,128,256]{2,1,0:T(8,128)(2,1)} %bitcast.19, bf16[1024,8192]{1,0:T(8,128)(2,1)} %w_hbm.1, bf16[16,2,16,1024]{3,2,1,0:T(8,128)(2,1)} %bitcast.20, bf16[16,2,16,256]{3,2,1,0:T(8,128)(2,1)} %bitcast.21, ...), custom_call_target="tpu_custom_call" | custom-call | flops 8858370048 | bytes 24117248 | tf_op jit(solution)/shard_map/pallas_call | solution.py:371
  95.5 1.4 %copy.20 = bf16[16,1024]{1,0:T(8,128)(2,1)} copy(bf16[16,1024]{1,0:T(8,128)(2,1)} %get-tuple-element.23) | data formatting | bytes 65536
  96.8 2.3 %copy.21 = bf16[512,1024]{1,0:T(8,128)(2,1)} copy(bf16[512,1024]{1,0:T(8,128)(2,1)} %bitcast.15) | data formatting | bytes 2097152
  (10 shorter events, 0.1 us)

commit v3 on v2

--- a/solution.py
+++ b/solution.py
@@ -11,45 +11,86 @@
 NEG = -1e30
 MESH = pl.DeviceIdType.MESH
 BF16, F32 = jnp.bfloat16, jnp.float32
+MAXIMUM = 2**30
 COLORS = 2
 CUTS = 2
+TOGETHER = 2
+FINAL, CONV, DEST, HIST, HIST_NAT, BACK, PAGES, PAGES_NAT = 0, 1, 2, 3, 4, 5, 8, 16
 CHIPS = 4
 
 
-def plan(page_table, hist_len, new_slot, engine_id, engines):
-    conv_dev = page_table.shape[0]
-    half = conv_dev // 2
-    slot = new_slot.reshape(engines, conv_dev)
-    target = slot // conv_dev
-    ids = jnp.arange(conv_dev, dtype=jnp.int32)
-    before = ids[None, :] < ids[:, None]
-    same = target[:, :, None] == target[:, None, :]
-    rank = jnp.sum(same & before, axis=2, dtype=jnp.int32)
-    doubled = jnp.sum(same, axis=2, dtype=jnp.int32) > 1
-    lone_before = jnp.sum(before[None] & ~doubled[:, None, :], axis=2, dtype=jnp.int32)
-    pairs = jnp.sum(doubled, axis=1, dtype=jnp.int32)[:, None] // 2
-    color = jnp.where(doubled, rank, (lone_before >= half - pairs).astype(jnp.int32))
-    place = jnp.sum((color[:, :, None] == color[:, None, :]) & before, axis=2, dtype=jnp.int32)
-    colors = jnp.arange(2, dtype=jnp.int32)
-    peers = jnp.arange(engines, dtype=jnp.int32)
-    out_mask = (target == engine_id)[None] & (color[None] == colors[:, None, None])
-    send = jnp.sum(jnp.where(out_mask, (slot % conv_dev)[None], 0), axis=2, dtype=jnp.int32).reshape(-1)
-    home = slot[None] == (engine_id * conv_dev + ids)[:, None, None]
-    final = jnp.sum(jnp.where(home, (color * engines + peers[:, None])[None], 0), axis=(1, 2), dtype=jnp.int32)
-    my_target = lax.dynamic_index_in_dim(target, engine_id, 0, False)
-    my_color = lax.dynamic_index_in_dim(color, engine_id, 0, False)
-    my_place = lax.dynamic_index_in_dim(place, engine_id, 0, False)
-    my_hist = lax.dynamic_slice_in_dim(hist_len, engine_id * conv_dev, conv_dev)
-    row = my_color * half + my_place
-    at = row[None, :] == ids[:, None]
-    pick = lambda v: jnp.sum(jnp.where(at, v[None], 0), axis=1, dtype=jnp.int32)
-    pages = jnp.sum(jnp.where(at[:, :, None], page_table[None], 0), axis=1, dtype=jnp.int32)
-    back_mask = (my_target[None] == peers[:, None])[None] & (my_color[None, None] == colors[:, None, None])
-    back = jnp.sum(jnp.where(back_mask, my_place[None, None], 0), axis=2, dtype=jnp.int32).reshape(-1)
-    return jnp.concatenate(
-        [send, back, final, pick(ids), pick(my_target), my_hist, pick(my_hist)]
-        + [page_table.reshape(-1), pages.reshape(-1)]
-    ).astype(jnp.int32)
+def plan(slot, hist, pages, me, engines, conv_dev, table):
+    half = conv_dev // COLORS
+    i32 = jnp.int32
+    lane = lax.broadcasted_iota(i32, slot.shape, 1)
+    local_id = lane % conv_dev
+    engine = lax.broadcasted_iota(i32, slot.shape, 0) * (128 // conv_dev) + lane // conv_dev
+    target, seat = slot // conv_dev, slot % conv_dev
+    zero = jnp.zeros(slot.shape, i32)
+
+    def earlier(v, d):
+        return pltpu.roll(v, d, 1), local_id >= d
+
+    def later(v, d):
+        return pltpu.roll(v, 128 - d, 1), local_id < conv_dev - d
+
+    rank, twins = zero, zero
+    for d in range(1, conv_dev):
+        v, ok = earlier(target, d)
+        rank = rank + jnp.where(ok & (v == target), 1, 0)
+        v, ok = later(target, d)
+        twins = twins + jnp.where(ok & (v == target), 1, 0)
+    doubled = jnp.where(rank + twins > 0, 1, 0)
+    ahead, behind = zero, zero
+    for d in range(1, conv_dev):
+        v, ok = earlier(doubled, d)
+        ahead = ahead + jnp.where(ok, v, 0)
+        v, ok = later(doubled, d)
+        behind = behind + jnp.where(ok, v, 0)
+    pairs = (ahead + doubled + behind) // 2
+    color = jnp.where(doubled > 0, rank, jnp.where(local_id - ahead >= half - pairs, 1, 0))
+    place = zero
+    for d in range(1, conv_dev):
+        v, ok = earlier(color, d)
+        place = place + jnp.where(ok & (v == color), 1, 0)
+    rows = slot.shape[0]
+    for c in range(COLORS):
+        v = jnp.where((target == me) & (color == c), seat, 0)
+        d = 1
+        while d < conv_dev:
+            v = v + pltpu.roll(v, 128 - d, 1)
+            d *= 2
+        table[16 + c * rows : 16 + (c + 1) * rows, :] = jnp.minimum(v, conv_dev - 1)
+    sub = lax.broadcasted_iota(i32, (conv_dev, 128), 0)
+
+    def gather(match, value):
+        total = jnp.zeros((conv_dev, 128), i32)
+        for r in range(rows):
+            hit = jnp.broadcast_to(match[r : r + 1], sub.shape) == sub
+            total = total + jnp.where(hit, jnp.broadcast_to(value[r : r + 1], sub.shape), 0)
+        return jnp.sum(total, axis=1, keepdims=True)
+
+    mine = engine == me
+    row = jnp.where(mine, color * half + place, -1)
+    conv = gather(row, local_id)
+    columns = [
+        gather(jnp.where(target == me, seat, -1), color * engines + engine),
+        conv,
+        gather(row, target),
+        gather(row, hist),
+        gather(jnp.where(mine, local_id, -1), hist),
+    ] + [gather(jnp.where(mine & (color == c), target, -1), place) for c in range(COLORS)]
+    wide = lax.broadcasted_iota(i32, (conv_dev, 128), 1)
+    result = jnp.zeros((conv_dev, 128), i32)
+    most = [COLORS * engines - 1, conv_dev - 1, engines - 1, MAXIMUM, MAXIMUM] + [half - 1] * COLORS
+    for c, (v, top) in enumerate(zip(columns, most)):
+        result = jnp.where(wide == c, jnp.clip(v, 0, top), result)
+    for p in range(pages.shape[0]):
+        line = jnp.broadcast_to(jnp.concatenate([pages[p : p + 1], jnp.zeros((1, 128 - conv_dev), i32)], axis=1), sub.shape)
+        by_row = jnp.sum(jnp.where(wide == conv, line, 0), axis=1, keepdims=True)
+        by_conv = jnp.sum(jnp.where(wide == sub, line, 0), axis=1, keepdims=True)
+        result = jnp.where(wide == PAGES + p, by_row, jnp.where(wide == PAGES_NAT + p, by_conv, result))
+    table[:16, :] = result
 
 
 def attend(queries, pages, fresh, bias, near, scale):
@@ -67,17 +108,17 @@
 
 
 def kernel(
-    tab, pool_hbm, w_hbm, tool_q, tool_kv, dec_q, dec_kv, out, dec_out,
-    pool, w, fsend, frecv_0, frecv_1, frecv_2, frecv_3, attn0, attn, heads, part0, part, got0, got, sums0, sums,
+    new_slot, hist_len, page_table, pool_hbm, w_hbm, tool_q, tool_kv, dec_q, dec_kv, out, dec_out,
+    table, tab, kv16, pool, w, fsend, frecv_0, frecv_1, frecv_2, frecv_3, attn0, attn, heads, part0, part, got0, got, sums0, sums,
     two0, two, direct0, direct, rows0, rows, bsend, brecv,
-    pool_sem, w_sem, fs, fr, xs, xr, ys, yr, bs, br,
+    tab_sem, pool_sem, w_sem, fs, fr, xs, xr, ys, yr, bs, br,
     *, engines, conv_dev, pages_max,
 ):
     stages = COLORS * CUTS
     frecv = [frecv_0, frecv_1, frecv_2, frecv_3]
     half = conv_dev // COLORS
     cut = tool_q.shape[2]
-    head = dec_q.shape[2]
+    head = pool.shape[2] // 2
     width = tool_q.shape[3]
     group = width // head
     page = pool.shape[1]
@@ -86,13 +127,6 @@
     width_out = w.shape[2]
     side = width_out // 2
     main = half * cut
-    SEND, BACK = 0, COLORS * engines
-    FINAL = BACK + COLORS * engines
-    CONV = FINAL + conv_dev
-    DEST = CONV + conv_dev
-    HIST = DEST + conv_dev
-    PAGES = HIST + 2 * conv_dev
-
     me, tp = lax.axis_index("engine"), lax.axis_index("tp")
     y, core = tp // 2, tp % 2
     partner = (me, y * 2 + 1 - core)
@@ -115,9 +149,19 @@
         pltpu.make_async_copy(w_hbm.at[:, pl.ds(b * width_out, width_out)], w.at[b], w_sem.at[b])
         for b in range(2 * CHIPS)
     ]
+    plan(new_slot[...], hist_len[...], page_table[...], me, engines, conv_dev, table)
+    load_tab = pltpu.make_async_copy(table, tab, tab_sem)
+    load_tab.start()
+    for h in range(group):
+        heads[h] = dec_q[:, h * head : (h + 1) * head].astype(F32)
+    dec_rows = dec_kv[...].astype(F32)
+    for i in range(conv_dev):
+        kv16[i] = jnp.broadcast_to(dec_rows[i : i + 1], (16, 2 * head)).astype(BF16)
+    load_tab.wait()
+    per_row = 128 // conv_dev
 
     def fill(ref, s, engine):
-        slot = tab[SEND + s // CUTS * engines + engine]
+        slot = tab[16 + s // CUTS * (engines // per_row) + engine // per_row, engine % per_row * conv_dev]
         ref[engine, :, :width] = tool_q[slot, s % CUTS]
         ref[engine, :, width:] = tool_kv[slot, s % CUTS]
 
@@ -150,11 +194,11 @@
     for copy in load_w:
         copy.start()
 
-    def pages_of(row):
-        return [pool[tab[PAGES + row * pages_max + p]] for p in range(pages_max)]
-
-    def bias_of(row):
-        return jnp.where(lax.broadcasted_iota(jnp.int32, (1, prefix), 1) < tab[HIST + row], 0.0, NEG)
+    def pages_of(row, first):
+        return [pool[tab[row, first + p]] for p in range(pages_max)]
+
+    def bias_of(row, column):
+        return jnp.where(lax.broadcasted_iota(jnp.int32, (1, prefix), 1) < tab[row, column], 0.0, NEG)
 
     col = lax.broadcasted_iota(jnp.int32, (16, page), 1)
     row = lax.broadcasted_iota(jnp.int32, (16, page), 0)
@@ -164,8 +208,9 @@
 
     @pl.loop(0, conv_dev)
     def _(i):
-        fresh = jnp.concatenate([dec_kv[i], jnp.zeros((page - 16, 2 * head), BF16)], axis=0)
-        got_i = attend(dec_q[i], pages_of(i), fresh, bias_of(i), only, scale)
+        fresh = jnp.concatenate([kv16[i], jnp.zeros((page - 16, 2 * head), BF16)], axis=0)
+        q = jnp.concatenate([heads[h, pl.ds(i, 1), :] for h in range(group)] + [jnp.zeros((16 - group, head), F32)], axis=0)
+        got_i = attend(q.astype(BF16), pages_of(i, PAGES_NAT), fresh, bias_of(i, HIST_NAT), only, scale)
         for h in range(group):
             heads[h, pl.ds(i, 1), :] = got_i[h : h + 1]
 
@@ -175,7 +220,7 @@
     def of(first, later, s):
         return first if s == 0 else later.at[s - 1]
 
-    def attention(s):
+    def attention(s, between):
         color, u = s // CUTS, s % CUTS
 
         @pl.loop(1, engines)
@@ -186,22 +231,30 @@
         near = jnp.where(((col <= row + u * cut) & (col < known)) | (col == known), 0.0, NEG)
         dst = of(attn0, attn, s)
 
-        @pl.loop(0, half)
-        def _(j):
-            conv = tab[CONV + color * half + j]
-            at = conv_dev + color * half + j
-            dest = tab[DEST + color * half + j]
+        def one(j):
+            at = color * half + j
+            conv, dest = tab[at, CONV], tab[at, DEST]
             kv_new = [frecv[color * CUTS + v][dest, :, width:] for v in range(u + 1)]
             fresh = jnp.concatenate(
-                kv_new + [dec_kv[conv], jnp.zeros((page - 16 - known, 2 * head), BF16)], axis=0
+                kv_new + [kv16[conv], jnp.zeros((page - 16 - known, 2 * head), BF16)], axis=0
             )
             q = frecv[s][dest, :, :width]
             queries = jnp.concatenate([q[:, h * head : (h + 1) * head] for h in range(group)], axis=0)
-            got_j = attend(queries, pages_of(at), fresh, bias_of(at), near, scale).astype(BF16)
-            for h in range(group):
-                dst[pl.ds(pl.multiple_of(j * cut, cut), cut), h * head : (h + 1) * head] = got_j[
-                    h * cut : (h + 1) * cut
-                ]
+            return attend(queries, pages_of(at, PAGES), fresh, bias_of(at, HIST), near, scale).astype(BF16)
+
+        def some(first, count):
+            @pl.loop(0, count // TOGETHER)
+            def _(i):
+                js = [first + i * TOGETHER + n for n in range(TOGETHER)]
+                for j, got_j in [(j, one(j)) for j in js]:
+                    for h in range(group):
+                        dst[pl.ds(pl.multiple_of(j * cut, cut), cut), h * head : (h + 1) * head] = got_j[
+                            h * cut : (h + 1) * cut
+                        ]
+
+        some(0, half // 2)
+        between()
+        some(half // 2, half // 2)
 
     def swap(s, k):
         return pltpu.make_async_remote_copy(
@@ -228,7 +281,7 @@
         mine, came, a = of(part0, part, s), of(got0, got, s), of(sums0, sums, s)
         for v in range(2):
             cols = slice(v * side, (v + 1) * side)
-            a[k, v] = (mine[2 * k + 1, :, cols].astype(F32) + came[k, :, cols].astype(F32)).astype(BF16)
+            a[k, v] = mine[2 * k + 1, :, cols] + came[k, :, cols]
 
     def project(s):
         src, dst = of(attn0, attn, s), of(part0, part, s)
@@ -268,7 +321,7 @@
         a, t, steps = of(sums0, sums, s), of(two0, two, s), ring(s)
         for v, k in ((0, 1), (1, 2)):
             steps[v].wait_recv()
-            a[k, v] = (a[k, v].astype(F32) + t[v].astype(F32)).astype(BF16)
+            a[k, v] = a[k, v] + t[v]
             steps[4 + v].start()
 
     def back(s, k):
@@ -296,7 +349,7 @@
             dst[:, :, v * side : (v + 1) * side] = total.reshape(-1, cut, side)
 
         def mine(engine):
-            place = tab[BACK + color * engines + engine]
+            place = tab[engine, BACK + color]
             return dst[place]
 
         @pl.loop(1, engines)
@@ -309,12 +362,10 @@
             dec_out[...] = dst[half]
 
     for s in range(stages):
-        attention(s)
+        attention(s, (lambda s=s: relay(s - 1)) if s > 0 else (lambda: None))
         if s == 0:
             for copy in load_w:
                 copy.wait()
-        else:
-            relay(s - 1)
         project(s)
         if s > 0:
             deliver(s - 1)
@@ -330,7 +381,7 @@
     @pl.loop(0, conv_dev)
     def _(n):
         for u in range(CUTS):
-            out[n, u] = brecv[u, tab[FINAL + n]]
+            out[n, u] = brecv[u, tab[n, FINAL]]
 
     for s in range(stages):
 
@@ -357,9 +408,6 @@
     side = width_out // 2
     stages = COLORS * CUTS
     main = conv_dev // COLORS * cut
-    tab = plan(page_table, hist_len, new_slot, lax.axis_index("engine"), engines)
-    dec16 = jnp.pad(dec_q.reshape(conv_dev, group, head), ((0, 0), (0, 16 - group), (0, 0)))
-    kv16 = jnp.broadcast_to(dec_kv, (conv_dev, 16, 2 * head))
     vmem = lambda shape: pltpu.VMEM(shape, BF16)
     split = lambda lead, cols: [
         vmem(lead + (main + conv_dev, cols)),
@@ -374,9 +422,12 @@
             jax.ShapeDtypeStruct((conv_dev, CUTS, cut, width_out), BF16),
             jax.ShapeDtypeStruct((conv_dev, width_out), BF16),
         ],
-        in_specs=[pl.BlockSpec(memory_space=pltpu.SMEM), anywhere, anywhere] + [in_vmem] * 4,
+        in_specs=[in_vmem] * 3 + [anywhere] * 2 + [in_vmem] * 4,
         out_specs=[in_vmem, in_vmem],
         scratch_shapes=[
+            pltpu.VMEM((24, 128), jnp.int32),
+            pltpu.SMEM((24, 128), jnp.int32),
+            vmem((conv_dev, 16, 2 * head)),
             vmem((kv_pool.shape[0], page, 2 * head)),
             vmem((2 * CHIPS, w_out.shape[0], width_out)),
             vmem((stages, engines, cut, width + 2 * head)),
@@ -392,6 +443,7 @@
             vmem((stages - 1, conv_dev // COLORS, cut, width_out)),
             vmem((stages, engines, cut, width_out)),
             vmem((CUTS, COLORS * engines, cut, width_out)),
+            dma(()),
             dma(()),
             dma((2 * CHIPS,)),
             dma((stages, engines)),
@@ -410,8 +462,9 @@
             flops=2 * (tool_rows + conv_dev) * w_out.size, bytes_accessed=2 * (w_out.size + kv_pool.size), transcendentals=0
         ),
     )(
-        tab, kv_pool[:, 0], w_out, tool_q.reshape(conv_dev, CUTS, cut, width),
-        tool_kv.reshape(conv_dev, CUTS, cut, 2 * head), dec16, kv16,
+        new_slot.reshape(-1, 128), hist_len.reshape(-1, 128), page_table.T, kv_pool[:, 0], w_out,
+        tool_q.reshape(conv_dev, CUTS, cut, width),
+        tool_kv.reshape(conv_dev, CUTS, cut, 2 * head), dec_q, dec_kv[:, 0],
     )
     return dec_out, tool_out.reshape(tool_rows, width_out)
 

time: 99.5 us -> 87.3 us (0.88)
  local copies, waits for them, and re-layouts: 9.78 us -> 3.64 us
  other arithmetic: 3.48 us -> 0 us
  Pallas kernels: 85.1 us -> 82.8 us
    reduce_sum x9 -> x0, other arithmetic: 3.32 us -> none  [the longest x1 0.9 us: plan(): jnp.sum(jnp.where(at[:, :, None], page_table[None], 0), axis=1, dtype=jnp...]
    pallas_call x1, Pallas kernels: 85.1 us -> 82.8 us  [local(): pl.pallas_call(functools.partial(kernel, engines=engines, conv_dev=conv_d...]
    unnamed x4 -> x2, local copies, waits for them, and re-layouts: 5.17 us -> 3.64 us
    broadcast_in_dim x1 -> x0, local copies, waits for them, and re-layouts: 1.36 us -> none  [local(): kv16 = jnp.broadcast_to(dec_kv, (conv_dev, 16, 2 * head))]
    reshape x5 -> x0, local copies, waits for them, and re-layouts: 1.1 us -> none  [the longest x1 0.75 us: plan(): slot = new_slot.reshape(engines, conv_dev)]
where the time goes in v3:
time: 87.3 us; the launch traced here: 87 us
  Pallas kernels  82.8 us (95%)
  local copies, waits for them, and re-layouts  3.64 us (4%)
    pallas_call x1, Pallas kernels, local(): pl.pallas_call(functools.partial(kernel, engines=engines, conv_dev=conv_d...  82.8 us
    unnamed x2, local copies, waits for them, and re-layouts  3.64 us

profile of v3, /device:TPU:0, one launch (start us, length us, event | category | flops | bytes accessed | tf_op | source)
XLA Modules:
  0.0 87.0 jit_solution(15538915575353361021)
XLA Ops:
  0.6 82.8 %shard_map.104 = (bf16[16,2,16,1024]{3,2,1,0:T(8,128)(2,1)}, bf16[16,1024]{1,0:T(8,128)(2,1)}) custom-call(s32[2,128]{1,0:T(2,128)} %bitcast.14, s32[2,128]{1,0:T(2,128)} %bitcast.15, s32[7,16]{1,0:T(8,128)} %bitcast.13, bf16[112,128,256]{2,1,0:T(8,128)(2,1)} %bitcast.9, bf16[1024,8192]{1,0:T(8,128)(2,1)} %w_hbm.1, bf16[16,2,16,1024]{3,2,1,0:T(8,128)(2,1)} %bitcast.10, ...), custom_call_target="tpu_custom_call" | custom-call | flops 8858370048 | bytes 24117248 | tf_op jit(solution)/shard_map/pallas_call | solution.py:419
  83.4 1.4 %copy.13 = bf16[16,1024]{1,0:T(8,128)(2,1)} copy(bf16[16,1024]{1,0:T(8,128)(2,1)} %get-tuple-element.8) | data formatting | bytes 65536
  84.8 2.3 %copy.14 = bf16[512,1024]{1,0:T(8,128)(2,1)} copy(bf16[512,1024]{1,0:T(8,128)(2,1)} %bitcast.8) | data formatting | bytes 2097152

commit v4 on v3

--- a/solution.py
+++ b/solution.py
@@ -14,7 +14,8 @@
 MAXIMUM = 2**30
 COLORS = 2
 CUTS = 2
-TOGETHER = 2
+TOKENS_TOGETHER = 4
+TOGETHER = 4
 FINAL, CONV, DEST, HIST, HIST_NAT, BACK, PAGES, PAGES_NAT = 0, 1, 2, 3, 4, 5, 8, 16
 CHIPS = 4
 
@@ -145,10 +146,21 @@
 
     load_pool = pltpu.make_async_copy(pool_hbm, pool, pool_sem)
     load_pool.start()
-    load_w = [
-        pltpu.make_async_copy(w_hbm.at[:, pl.ds(b * width_out, width_out)], w.at[b], w_sem.at[b])
-        for b in range(2 * CHIPS)
-    ]
+
+    def block_at(b):
+        k = b // 2
+        far = lax.rem(2 - k - k // 2 + 2 * (k // 3) + y + CHIPS, CHIPS)
+        return far * 2 + lax.rem(core + 1 + b % 2, 2)
+
+    def load_w(b):
+        block = block_at(b)
+        columns = pl.ds(pl.multiple_of(block * width_out, width_out), width_out)
+        return pltpu.make_async_copy(w_hbm.at[:, columns], w.at[block], w_sem.at[block])
+
+    @pl.loop(0, 2 * CHIPS)
+    def _(b):
+        load_w(b).start()
+
     plan(new_slot[...], hist_len[...], page_table[...], me, engines, conv_dev, table)
     load_tab = pltpu.make_async_copy(table, tab, tab_sem)
     load_tab.start()
@@ -177,22 +189,24 @@
             device_id=(other(k), tp), device_id_type=MESH,
         )
 
-    for s in range(stages):
-
+    def dispatch(s):
         @pl.loop(1, engines)
-        def _(k, s=s):
+        def _(k):
             fill(fsend.at[s], s, other(k))
 
         if s == 0:
             pl.semaphore_wait(barrier, engines - 1 + 3)
 
         @pl.loop(1, engines)
-        def _(k, s=s):
+        def _(k):
             fwd(s, k).start()
 
         fill(frecv[s], s, me)
-    for copy in load_w:
-        copy.start()
+
+    dispatch(0)
+    dispatch(1)
+    dispatch(2)
+    dispatch(3)
 
     def pages_of(row, first):
         return [pool[tab[row, first + p]] for p in range(pages_max)]
@@ -206,13 +220,20 @@
     load_pool.wait()
     only = jnp.where(col == 0, 0.0, NEG)
 
-    @pl.loop(0, conv_dev)
-    def _(i):
-        fresh = jnp.concatenate([kv16[i], jnp.zeros((page - 16, 2 * head), BF16)], axis=0)
-        q = jnp.concatenate([heads[h, pl.ds(i, 1), :] for h in range(group)] + [jnp.zeros((16 - group, head), F32)], axis=0)
-        got_i = attend(q.astype(BF16), pages_of(i, PAGES_NAT), fresh, bias_of(i, HIST_NAT), only, scale)
-        for h in range(group):
-            heads[h, pl.ds(i, 1), :] = got_i[h : h + 1]
+    def decode(step):
+        at = [step * TOKENS_TOGETHER + n for n in range(TOKENS_TOGETHER)]
+        results = []
+        for i in at:
+            fresh = jnp.concatenate([kv16[i], jnp.zeros((page - 16, 2 * head), BF16)], axis=0)
+            q = jnp.concatenate(
+                [heads[h, pl.ds(i, 1), :] for h in range(group)] + [jnp.zeros((16 - group, head), F32)], axis=0
+            )
+            results.append(attend(q.astype(BF16), pages_of(i, PAGES_NAT), fresh, bias_of(i, HIST_NAT), only, scale))
+        for i, got_i in zip(at, results):
+            for h in range(group):
+                heads[h, pl.ds(i, 1), :] = got_i[h : h + 1]
+
+    pl.loop(0, conv_dev // TOKENS_TOGETHER)(decode)
 
     for h in range(group):
         attn0[main:, h * head : (h + 1) * head] = heads[h].astype(BF16)
@@ -289,9 +310,9 @@
 
         @pl.loop(0, 2 * CHIPS)
         def _(b):
-            k = b // 2
-            far = lax.rem(2 - k - k // 2 + 2 * (k // 3) + y + CHIPS, CHIPS)
-            block = far * 2 + lax.rem(core + 1 + b % 2, 2)
+            k, block = b // 2, block_at(b)
+            if s == 0:
+                load_w(b).wait()
             dst[b] = jnp.dot(src[...], w[block], preferred_element_type=F32).astype(BF16)
 
             @pl.when(b % 2 == 0)
@@ -363,9 +384,6 @@
 
     for s in range(stages):
         attention(s, (lambda s=s: relay(s - 1)) if s > 0 else (lambda: None))
-        if s == 0:
-            for copy in load_w:
-                copy.wait()
         project(s)
         if s > 0:
             deliver(s - 1)

time: 87.3 us -> 86.6 us (level)
  no operation moved by 1% of the time
where the time goes in v4:
time: 86.6 us; the launch traced here: 86.3 us
  Pallas kernels  82.1 us (95%)
  local copies, waits for them, and re-layouts  3.64 us (4%)
    pallas_call x1, Pallas kernels, local(): pl.pallas_call(functools.partial(kernel, engines=engines, conv_dev=conv_d...  82.1 us
    unnamed x2, local copies, waits for them, and re-layouts  3.64 us

profile of v4, /device:TPU:0, one launch (start us, length us, event | category | flops | bytes accessed | tf_op | source)
XLA Modules:
  0.0 86.3 jit_solution(2538497868758795560)
XLA Ops:
  0.6 82.1 %shard_map.104 = (bf16[16,2,16,1024]{3,2,1,0:T(8,128)(2,1)}, bf16[16,1024]{1,0:T(8,128)(2,1)}) custom-call(s32[2,128]{1,0:T(2,128)} %bitcast.14, s32[2,128]{1,0:T(2,128)} %bitcast.15, s32[7,16]{1,0:T(8,128)} %bitcast.13, bf16[112,128,256]{2,1,0:T(8,128)(2,1)} %bitcast.9, bf16[1024,8192]{1,0:T(8,128)(2,1)} %w_hbm.1, bf16[16,2,16,1024]{3,2,1,0:T(8,128)(2,1)} %bitcast.10, ...), custom_call_target="tpu_custom_call" | custom-call | flops 8858370048 | bytes 24117248 | tf_op jit(solution)/shard_map/pallas_call | solution.py:437
  82.7 1.4 %copy.13 = bf16[16,1024]{1,0:T(8,128)(2,1)} copy(bf16[16,1024]{1,0:T(8,128)(2,1)} %get-tuple-element.8) | data formatting | bytes 65536
  84.1 2.3 %copy.14 = bf16[512,1024]{1,0:T(8,128)(2,1)} copy(bf16[512,1024]{1,0:T(8,128)(2,1)} %bitcast.8) | data formatting | bytes 2097152

commit v5 on v4

--- a/solution.py
+++ b/solution.py
@@ -133,7 +133,7 @@
     partner = (me, y * 2 + 1 - core)
     up = (me, (y + 1) % CHIPS * 2 + core)
     down = (me, (y + CHIPS - 1) % CHIPS * 2 + core)
-    other = lambda k: lax.rem(me + k, engines)
+    other = lambda k: lax.rem(me + 7 * k, engines)
 
     barrier = pltpu.get_barrier_semaphore()
 

time: 86.6 us -> 85.8 us (level)
  Pallas kernels: 82.1 us -> 81.1 us
    pallas_call x1, Pallas kernels: 82.1 us -> 81.1 us  [local(): pl.pallas_call(functools.partial(kernel, engines=engines, conv_dev=conv_d...]
where the time goes in v5:
time: 85.8 us; the launch traced here: 85.4 us
  Pallas kernels  81.1 us (95%)
  local copies, waits for them, and re-layouts  3.64 us (4%)
    pallas_call x1, Pallas kernels, local(): pl.pallas_call(functools.partial(kernel, engines=engines, conv_dev=conv_d...  81.1 us
    unnamed x2, local copies, waits for them, and re-layouts  3.64 us

profile of v5, /device:TPU:0, one launch (start us, length us, event | category | flops | bytes accessed | tf_op | source)
XLA Modules:
  0.0 85.4 jit_solution(17663911540987992773)
XLA Ops:
  0.6 81.1 %shard_map.104 = (bf16[16,2,16,1024]{3,2,1,0:T(8,128)(2,1)}, bf16[16,1024]{1,0:T(8,128)(2,1)}) custom-call(s32[2,128]{1,0:T(2,128)} %bitcast.14, s32[2,128]{1,0:T(2,128)} %bitcast.15, s32[7,16]{1,0:T(8,128)} %bitcast.13, bf16[112,128,256]{2,1,0:T(8,128)(2,1)} %bitcast.9, bf16[1024,8192]{1,0:T(8,128)(2,1)} %w_hbm.1, bf16[16,2,16,1024]{3,2,1,0:T(8,128)(2,1)} %bitcast.10, ...), custom_call_target="tpu_custom_call" | custom-call | flops 8858370048 | bytes 24117248 | tf_op jit(solution)/shard_map/pallas_call | solution.py:437
  81.8 1.4 %copy.13 = bf16[16,1024]{1,0:T(8,128)(2,1)} copy(bf16[16,1024]{1,0:T(8,128)(2,1)} %get-tuple-element.8) | data formatting | bytes 65536
  83.1 2.3 %copy.14 = bf16[512,1024]{1,0:T(8,128)(2,1)} copy(bf16[512,1024]{1,0:T(8,128)(2,1)} %bitcast.8) | data formatting | bytes 2097152
